TPU v7x, 256 devices: a whole 4x4x8 slice. The times are simulated.
256 devices in a mesh: long: 16 (over y, x_hi, core), inner: 16 (over x_lo, z).
Axes of the slice: x: 4 (x_hi: 2, x_lo: 2; x = x_hi * 2 + x_lo), y: 4, z: 8, core: 2. Of those that a mesh axis runs over, the one named last changes fastest.
Arguments:
- image_raw: bfloat16 [16384, 1280], P(('long', 'inner')), may hold values from -1 to 1, as said below
- text_raw: bfloat16 [16384, 1280], P(('long', 'inner')), may hold values from -1 to 1, as said below
- log_scale: float32 [1], replicated, may hold values from 4 to 4.6
Outputs:
- grad_image: bfloat16 [16384, 1280], P(('long', 'inner'))
- grad_text: bfloat16 [16384, 1280], P(('long', 'inner'))
- loss: float32 [1], replicated
- grad_log_scale: float32 [1], replicated
Inputs may be any that keep to these rules, and one draw needn't show every extreme that they name: `image_raw`: each image row and its paired text row are partly aligned. `text_raw`: each text row and its paired image row are partly aligned.
All inputs are finite; a program needn't handle non-finite values.
Results may differ from a plain program's by a relative error of at most 0.017.
Values may be sent and summed in bfloat16 or wider, within the bound.
No kernel may reach another device: no remote copies, remote signals or barrier semaphores. Data moves between devices by JAX's collectives and lax.ppermute only.
A program may use at most 64 MiB of HBM per device.

v0:
```python
import jax
import jax.numpy as jnp
from jax import lax
from jax.sharding import PartitionSpec as P

NORM_EPS = 1e-06


def normalize(raw_rows):
    values = raw_rows.astype(jnp.float32)
    inv_norm = 1.0 / jnp.sqrt(jnp.sum(values * values, axis=1, keepdims=True) + NORM_EPS)
    return (values * inv_norm, inv_norm)


def unnormalize(grad_hat, unit_rows, inv_norm):
    inner_prod = jnp.sum(grad_hat * unit_rows, axis=1, keepdims=True)
    return (inv_norm * (grad_hat - unit_rows * inner_prod)).astype(jnp.bfloat16)


def summaries(logits, peak_values, along):
    shifted = jnp.exp(logits - peak_values)
    sum_exp = jnp.sum(shifted, axis=along)
    return sum_exp[None, :]


def per_device(image_raw, text_raw, log_scale):
    img_unit, img_norm = normalize(image_raw)
    txt_unit, txt_norm = normalize(text_raw)
    img_hat = img_unit.astype(jnp.bfloat16)
    txt_hat = txt_unit.astype(jnp.bfloat16)
    row_count = img_hat.shape[0]
    img_rows = lax.all_gather(img_hat, "inner", axis=0, tiled=True)
    txt_cols = lax.all_gather(txt_hat, "long", axis=0, tiled=True)
    row_start = lax.axis_index("inner") * row_count
    col_start = lax.axis_index("long") * row_count
    logit_mult = jnp.exp(log_scale[0])
    logits = logit_mult * lax.dot_general(
        img_rows, txt_cols, (((1,), (1,)), ((), ())), preferred_element_type=jnp.float32
    )
    row_ids = lax.broadcasted_iota(jnp.int32, logits.shape, 0) - row_start
    col_ids = lax.broadcasted_iota(jnp.int32, logits.shape, 1) - col_start
    identity_mask = ((row_ids == col_ids) & (row_ids >= 0) & (row_ids < row_count)).astype(
        jnp.float32
    )
    row_peak = jnp.max(logits, axis=1)
    col_peak = jnp.max(logits, axis=0)
    row_peak = lax.pmax(row_peak, "inner")
    col_peak = lax.pmax(col_peak, "long")
    row_parts = lax.psum(summaries(logits, row_peak[:, None], 1), "inner")
    col_parts = lax.psum(summaries(logits, col_peak[None, :], 0), "long")
    lse_row = row_peak + jnp.log(row_parts[0])
    lse_col = col_peak + jnp.log(col_parts[0])
    diag_all = jnp.sum(logits * identity_mask, axis=1)
    diag_own = lax.dynamic_slice_in_dim(diag_all, row_start, row_count)
    lse_row_own = lax.dynamic_slice_in_dim(lse_row, row_start, row_count)
    lse_col_own = lax.dynamic_slice_in_dim(lse_col, col_start, row_count)
    loss_part = jnp.sum(lse_row_own - diag_own) + jnp.sum(lse_col_own - diag_own)
    batch_total = img_rows.shape[0] * txt_cols.shape[0] // row_count
    dlogits = (
        0.5 * jnp.exp(logits - lse_row[:, None])
        + 0.5 * jnp.exp(logits - lse_col[None, :])
        - identity_mask
    )
    dlogits_b = dlogits.astype(jnp.bfloat16)
    grad_img_hat = lax.psum_scatter(
        (logit_mult * jnp.dot(dlogits_b, txt_cols, preferred_element_type=jnp.float32)).astype(
            jnp.bfloat16
        ),
        "inner",
        scatter_dimension=0,
        tiled=True,
    ).astype(jnp.float32)
    grad_txt_hat = lax.psum_scatter(
        (
            logit_mult
            * lax.dot_general(
                dlogits_b, img_rows, (((0,), (0,)), ((), ())), preferred_element_type=jnp.float32
            )
        ).astype(jnp.bfloat16),
        "long",
        scatter_dimension=0,
        tiled=True,
    ).astype(jnp.float32)
    slope_part = jnp.sum(dlogits * logits)
    loss_sum, slope_sum = lax.psum((loss_part, slope_part), ("long", "inner"))
    loss_value = loss_sum / (2 * batch_total)
    scale_grad = slope_sum / batch_total
    grad_image = unnormalize(grad_img_hat, img_unit, img_norm)
    grad_text = unnormalize(grad_txt_hat, txt_unit, txt_norm)
    return (grad_image, grad_text, jnp.reshape(loss_value, (1,)), jnp.reshape(scale_grad, (1,)))


def solution(mesh):
    in_specs = (P(("long", "inner"), None), P(("long", "inner"), None), P())
    out_specs = (P(("long", "inner"), None), P(("long", "inner"), None), P(), P())
    return jax.shard_map(
        per_device, mesh=mesh, in_specs=in_specs, out_specs=out_specs, check_vma=False
    )
```

profile of v0, /device:TPU:16, one launch (start us, length us, event | category | flops | bytes accessed | tf_op | source)
XLA Modules:
  0.0 458.9 jit_solution(596900744115289861)
XLA Ops:
  7.2 0.0 all-gather.5.cloned.1.call-start
  7.2 1.0 fusion.6
  8.3 1.7 fusion.2
  10.0 0.0 all-gather.5.cloned.1.call-update
  10.0 0.0 all-gather.3.cloned.1.call-start
  10.0 1.0 fusion.5
  11.1 1.7 fusion.4
  12.8 0.0 all-gather.3.cloned.1.call-update
  12.8 0.0 reduce-scatter.5.cloned.1.call-start
  13.6 53.2 %all-gather.5.cloned.1.call-done = bf16[1024,1280]{1,0:T(8,128)(2,1)} async-done(((bf16[64,1280]{1,0:T(8,128)(2,1)}), bf16[1024,1280]{1,0:T(8,128)(2,1)}) %all-gather.5.cloned.1.call-update) | async-done | bytes 2621456 | tf_op jit(solution)/shard_map/all_gather | solution.py:33
  66.8 76.0 %all-gather.3.cloned.1.call-done = bf16[1024,1280]{1,0:T(8,128)(2,1)} async-done(((bf16[64,1280]{1,0:T(8,128)(2,1)}), bf16[1024,1280]{1,0:T(8,128)(2,1)}) %all-gather.3.cloned.1.call-update) | async-done | bytes 2621456 | tf_op jit(solution)/shard_map/all_gather | solution.py:32
  142.8 7.4 %multiply_reduce_fusion.2 = (f32[1024]{0:T(1024)S(1)}, f32[1024,1024]{0,1:T(8,128)}) fusion(f32[]{:T(128)} %bitcast, bf16[1024,1280]{1,0:T(8,128)(2,1)} %all-gather.3.cloned.1.call-done, bf16[1024,1280]{1,0:T(8,128)(2,1)} %all-gather.5.cloned.1.call-done), kind=kOutput, calls=%fused_computation.10 | convolution fusion | flops 2686450688 | bytes 9441284 | tf_op jit(solution)/shard_map/dot_general | solution.py:37
  150.2 33.6 %pmax.14 = f32[1024]{0:T(1024)S(1)} all-reduce(f32[1024]{0:T(1024)S(1)} %get-tuple-element.12), channel_id=1, replica_groups=mesh['long'=16,'inner'=16] {'inner'}, use_global_device_ids=true, to_apply=%region_3.0 | all-reduce | flops 1024 | bytes 8192 | tf_op jit(solution)/shard_map/pmax | solution.py:47
  183.7 3.1 exponential_reduce_fusion.1
  186.8 30.6 %psum.28 = f32[1,1024]{1,0:T(1,128)S(1)} all-reduce(f32[1,1024]{1,0:T(1,128)S(1)} %bitcast.11), channel_id=1, replica_groups=mesh['long'=16,'inner'=16] {'inner'}, use_global_device_ids=true, to_apply=%region_5.0 | all-reduce | flops 1024 | bytes 8192 | tf_op jit(solution)/shard_map/psum | solution.py:49
  217.5 28.3 %pmax.15 = f32[1024]{0:T(1024)S(1)} all-reduce(f32[1024]{0:T(1024)S(1)} %get-tuple-element.7), channel_id=1, replica_groups=mesh['long'=16,'inner'=16] {'long'}, use_global_device_ids=true, to_apply=%region_7.0 | all-reduce | flops 1024 | bytes 8192 | tf_op jit(solution)/shard_map/pmax | solution.py:48
  245.8 3.0 exponential_reduce_fusion
  248.9 28.3 %psum.29 = f32[1,1024]{1,0:T(1,128)S(1)} all-reduce(f32[1,1024]{1,0:T(1,128)S(1)} %bitcast.14), channel_id=1, replica_groups=mesh['long'=16,'inner'=16] {'long'}, use_global_device_ids=true, to_apply=%region_9.0 | all-reduce | flops 1024 | bytes 8192 | tf_op jit(solution)/shard_map/psum | solution.py:50
  277.2 0.0 copy-start.2
  277.2 9.2 %multiply_convert_fusion = bf16[1024,1280]{1,0:T(8,128)(2,1)} fusion(bf16[1024,1280]{1,0:T(8,128)(2,1)} %all-gather.3.cloned.1.call-done, f32[]{:T(128)} %bitcast, f32[1024,1024]{0,1:T(8,128)} %get-tuple-element.13, s32[1024]{0:T(1024)S(1)} %get-tuple-element.17, f32[1024]{0:T(1024)S(1)} %add.51, f32[1024]{0:T(1024)S(1)} %add.50, ...), kind=kOutput, calls=%fused_computation | convolution fusion | flops 2698510336 | bytes 9455620 | tf_op jit(solution)/shard_map/dot_general | solution.py:76
  286.4 0.0 reduce-scatter.5.cloned.1.call-update
  286.5 0.2 reduce-scatter.3.cloned.1.call-start
  286.7 0.0 copy-done.2
  286.7 8.0 %multiply_convert_fusion.1 = bf16[1024,1280]{1,0:T(8,128)(2,1)} fusion(bf16[1024,1280]{1,0:T(8,128)(2,1)S(1)} %copy-done.2, f32[]{:T(128)} %bitcast, f32[1024,1024]{0,1:T(8,128)} %get-tuple-element.13, s32[1024]{0:T(1024)S(1)} %get-tuple-element.17, f32[1024]{0:T(1024)S(1)} %add.51, f32[1024]{0:T(1024)S(1)} %add.50, s32[1024]{0:T(1024)S(1)} %get-tuple-element.16, ...), kind=kOutput, calls=%fused_computation.1 | convolution fusion | flops 2698510336 | bytes 9455620 | tf_op jit(solution)/shard_map/dot_general | solution.py:66
  294.7 0.0 copy-start
  294.7 0.0 copy-start.1
  294.7 0.0 reduce-scatter.3.cloned.1.call-update
  294.7 6.1 %multiply_reduce_fusion = (f32[]{:T(128)}, f32[1024]{0:T(1024)S(1)}) fusion(f32[1024,1024]{0,1:T(8,128)} %get-tuple-element.13, s32[1024]{0:T(1024)S(1)} %get-tuple-element.17, f32[1024]{0:T(1024)S(1)} %add.51, f32[1024]{0:T(1024)S(1)} %add.50, f32[]{:T(128)} %bitcast, s32[1024]{0:T(1024)S(1)} %get-tuple-element.16, ...), kind=kLoop, calls=%fused_computation.2 | loop fusion | flops 14679039 | bytes 4216840 | tf_op jit(solution)/shard_map/reduce_sum | solution.py:84
  300.8 0.7 subtract_reduce_fusion
  302.8 82.5 %all-reduce = (f32[]{:T(128)}, f32[]{:T(128)}) all-reduce(f32[]{:T(128)S(6)} %add.55, f32[]{:T(128)} %get-tuple-element.4), channel_id=1, replica_groups=mesh['long'=16,'inner'=16] {'long','inner'}, use_global_device_ids=true, to_apply=%region_17.0 | all-reduce | flops 2 | bytes 16 | tf_op jit(solution)/shard_map/psum | solution.py:85
  386.6 0.0 reduce-scatter.5.cloned.1.call-done
  386.6 0.0 copy-done
  386.6 1.1 fusion.10
  387.8 1.7 fusion.12
  389.5 57.6 %reduce-scatter.3.cloned.1.call-done = bf16[64,1280]{1,0:T(8,128)(2,1)} async-done(((bf16[1024,1280]{1,0:T(8,128)(2,1)}), bf16[64,1280]{1,0:T(8,128)(2,1)}) %reduce-scatter.3.cloned.1.call-update) | async-done | bytes 163856 | tf_op jit(solution)/shard_map/reduce_scatter | solution.py:65
  447.2 0.0 copy-done.1
  447.2 1.1 fusion.7
  448.3 1.7 fusion.9
  (8 shorter events, 0.1 us)
Async XLA Ops:
  7.2 59.6 %all-gather.5.cloned.1.call-start = ((), (), s32[]{:S(2)}) async-start(), calls=%async_computation.3 | async-start | bytes 2785280 | tf_op jit(solution)/shard_map/all_gather | solution.py:33
  10.0 132.8 %all-gather.3.cloned.1.call-start = ((), (), s32[]{:S(2)}) async-start(), calls=%async_computation.2 | async-start | bytes 2785280 | tf_op jit(solution)/shard_map/all_gather | solution.py:32
  12.8 373.8 %reduce-scatter.5.cloned.1.call-start = ((), (), s32[]{:S(2)}) async-start(), calls=%async_computation.5 | async-start | bytes 2785280 | tf_op jit(solution)/shard_map/reduce_scatter | solution.py:73
  277.2 9.5 %copy-start.2 = (bf16[1024,1280]{1,0:T(8,128)(2,1)S(1)}, bf16[1024,1280]{1,0:T(8,128)(2,1)}, u32[]{:S(2)}) copy-start(bf16[1024,1280]{1,0:T(8,128)(2,1)} %all-gather.5.cloned.1.call-done) | copy-start | bytes 7864324
  286.5 160.7 %reduce-scatter.3.cloned.1.call-start = ((), (), s32[]{:S(2)}) async-start(), calls=%async_computation.4 | async-start | bytes 2785280 | tf_op jit(solution)/shard_map/reduce_scatter | solution.py:65
  294.7 91.9 %copy-start = (bf16[64,1280]{1,0:T(8,128)(2,1)S(1)}, bf16[64,1280]{1,0:T(8,128)(2,1)}, u32[]{:S(2)}) copy-start(bf16[64,1280]{1,0:T(8,128)(2,1)} %param.4) | copy-start | bytes 491524
  294.7 152.5 %copy-start.1 = (bf16[64,1280]{1,0:T(8,128)(2,1)S(1)}, bf16[64,1280]{1,0:T(8,128)(2,1)}, u32[]{:S(2)}) copy-start(bf16[64,1280]{1,0:T(8,128)(2,1)} %param.3) | copy-start | bytes 491524
Sparse Core Ops, SparseCore 0:
  11.3 55.4 all-gather.4
  69.1 73.6 all-gather.2
  286.6 81.7 reduce-scatter.4
  370.8 76.3 reduce-scatter.2
where the time goes:
time: 459 us
  blocking collectives  203 us (44%)
  waiting for transfers between devices  187 us (41%)
  matrix products  24.6 us (5%)
  other arithmetic  24.2 us (5%)
  between operations  19.4 us (4%)
    psum x1, blocking collectives, per_device(): loss_sum, slope_sum = lax.psum((loss_part, slope_part), ('long', 'inner'))  82.5 us
    all_gather x1, waiting for transfers between devices, per_device(): img_rows = lax.all_gather(img_hat, 'inner', axis=0, tiled=True)  76 us
    reduce_scatter x1, waiting for transfers between devices, per_device(): lax.psum_scatter((logit_mult * jnp.dot(dlogits_b, txt_cols, preferred_ele...  57.6 us
    all_gather x1, waiting for transfers between devices, per_device(): txt_cols = lax.all_gather(txt_hat, 'long', axis=0, tiled=True)  53.2 us
    pmax x1, blocking collectives, per_device(): row_peak = lax.pmax(row_peak, 'inner')  33.6 us
    psum x1, blocking collectives, per_device(): row_parts = lax.psum(summaries(logits, row_peak[:, None], 1), 'inner')  30.6 us
    pmax x1, blocking collectives, per_device(): col_peak = lax.pmax(col_peak, 'long')  28.3 us
    psum x1, blocking collectives, per_device(): col_parts = lax.psum(summaries(logits, col_peak[None, :], 0), 'long')  28.3 us
  transfers between devices with their start and end apart: 4, of which 3 were waited for; matrix products, arithmetic and copies ran while one was open for 4% of the time, Pallas kernels for 0%

commit v1 on v0

v1 whole, which is shorter than its diff:
```python
import functools
import itertools

import jax
import jax.numpy as jnp
from jax import lax
from jax.experimental import pallas as pl
from jax.experimental.pallas import tpu as pltpu
from jax.sharding import Mesh, PartitionSpec as P

NORM_EPS = 1e-06
AXES = ("y", "xh", "c", "xl", "z")
SIZES = (4, 2, 2, 2, 8)
PLANE = ("y", "xh", "xl")
LINE = ("c", "z")
GROUP = 16
VMEM_LIMIT = 48 * 1024 * 1024
F32 = jnp.float32
BF16 = jnp.bfloat16


def params():
    return pltpu.CompilerParams(vmem_limit_bytes=VMEM_LIMIT)


def whole(space=pltpu.VMEM):
    return pl.BlockSpec(memory_space=space)


def permute(array, move):
    pairs = []
    for y, xh, c, xl, z in itertools.product(*map(range, SIZES)):
        x, y2, z2, c2 = move(2 * xh + xl, y, z, c)
        x, y2, z2, c2 = x % 4, y2 % 4, z2 % 8, c2 % 2
        flat = lambda y, x, z, c: (((y * 2 + x // 2) * 2 + c) * 2 + x % 2) * 8 + z
        pairs.append((flat(y, 2 * xh + xl, z, c), flat(y2, x, z2, c2)))
    return lax.ppermute(array, AXES, pairs)


def plane_step(step, turned):
    def move(x, y, z, c):
        return (x + step, y, z, c) if (c == 0) != turned else (x, y + step, z, c)

    return move


def ring_gather(block, turned):
    half = block.shape[0] // 2
    below = permute(block, plane_step(1, turned))
    above = permute(block, plane_step(-1, turned))
    far_low = permute(below[:half], plane_step(1, turned))
    far_high = permute(above[half:], plane_step(-1, turned))
    return [block, below, above, far_low, far_high]


def normalize_kernel(img_ref, txt_ref, img_hat_ref, txt_hat_ref, diag_ref):
    hats = []
    for raw, hat in ((img_ref, img_hat_ref), (txt_ref, txt_hat_ref)):
        values = raw[...].astype(F32)
        recip = 1.0 / jnp.sqrt(jnp.sum(values * values, axis=1, keepdims=True) + NORM_EPS)
        hat[...] = (values * recip).astype(BF16)
        hats.append(hat[...].astype(F32))
    diag = jnp.sum(hats[0] * hats[1])
    diag_ref[...] = jnp.full(diag_ref.shape, diag, F32)


def rows_of(vector):
    return jnp.concatenate([vector[:, k * 128 : (k + 1) * 128] for k in range(8)], axis=0)


def lanes_of(rows):
    return jnp.concatenate([rows[k : k + 1, :] for k in range(8)], axis=1)


def logits_kernel(tile, place_ref, scale_ref, img_ref, t0, t1, t2, t3, t4, txt_ref, logit_ref, row_ref, col_ref, txt_all, row_acc):
    step = pl.program_id(0)
    steps = pl.num_programs(0)

    @pl.when(step == 0)
    def _():
        pieces = [(t0, 0), (t0, 1), (t0, 2), (t0, 3), (t1, 0), (t1, 1), (t1, 2), (t1, 3)]
        pieces += [(t2, 0), (t2, 1), (t2, 2), (t2, 3), (t3, 0), (t3, 1), (t4, 0), (t4, 1)]
        for k, (ref, at) in enumerate(pieces):
            start = pl.multiple_of(place_ref[k] * 64, 64)
            txt_all[pl.ds(start, 64), :] = ref[at * 64 : (at + 1) * 64, :]
        txt_ref[...] = txt_all[...]
        row_acc[...] = jnp.zeros_like(row_acc)

    scale = scale_ref[0]
    shift = scale_ref[1]
    start = pl.multiple_of(step * tile, tile)
    block = txt_all[pl.ds(start, tile), :]
    logits = scale * lax.dot_general(img_ref[...], block, (((1,), (1,)), ((), ())), preferred_element_type=F32)
    logit_ref[...] = logits
    powers = jnp.exp(logits - shift)
    weighted = powers * logits
    for k in range(tile // 128):
        row_acc[0] += powers[:, k * 128 : (k + 1) * 128]
        row_acc[1] += weighted[:, k * 128 : (k + 1) * 128]
    sums = jnp.sum(powers, axis=0, keepdims=True)
    slopes = jnp.sum(weighted, axis=0, keepdims=True)
    rows = tile // 128
    for k in range(rows):
        for copy in range(GROUP):
            col_ref[copy, pl.ds(step * rows + k, 1), :] = sums[:, k * 128 : (k + 1) * 128]
            col_ref[copy, pl.ds(8 + step * rows + k, 1), :] = slopes[:, k * 128 : (k + 1) * 128]

    @pl.when(step == steps - 1)
    def _():
        row_ref[0:8, :] = rows_of(jnp.sum(row_acc[0].T, axis=0, keepdims=True))
        row_ref[8:16, :] = rows_of(jnp.sum(row_acc[1].T, axis=0, keepdims=True))


def column_kernel(col_ref, row_ref, diag_ref, send_ref, sums_ref):
    total = jnp.sum(col_ref[...], axis=0)
    sums, slopes = total[0:8], total[8:16]
    sums_ref[...] = sums
    log_sum = jnp.sum(jnp.log(sums))
    slope_sum = 0.5 * jnp.sum(slopes / sums)
    lane = lax.broadcasted_iota(jnp.int32, (8, 128), 1)
    scalars = jnp.where(lane == 0, log_sum, jnp.where(lane == 1, slope_sum, diag_ref[...]))
    for copy in range(GROUP):
        send_ref[copy, 0:16, :] = row_ref[...]
        send_ref[copy, 16:24, :] = scalars


def image_kernel(tile, core_ref, shift_ref, logit_ref, txt_ref, recv_ref, sums_ref, keep_ref, send_ref, dlogit_ref, scalar_ref, row_half, col_half):
    step = pl.program_id(0)

    @pl.when(step == 0)
    def _():
        total = jnp.sum(recv_ref[...], axis=0)
        sums, slopes, others = total[0:8], total[8:16], total[16:24]
        log_sum = jnp.sum(jnp.log(sums))
        slope_sum = 0.5 * jnp.sum(slopes / sums)
        lane = lax.broadcasted_iota(jnp.int32, (8, 128), 1)
        row = lax.broadcasted_iota(jnp.int32, (8, 128), 0)
        own = jnp.where(lane == 0, log_sum, jnp.where(lane == 1, slope_sum, others))
        scalar_ref[...] = jnp.where(row == 0, others, own)
        row_half[...] = jnp.broadcast_to(lanes_of(0.5 / sums), (128, 1024)).T
        col_half[...] = lanes_of(0.5 / sums_ref[...])

    start = pl.multiple_of(step * tile, tile)
    powers = jnp.exp(logit_ref[...] - shift_ref[1])
    by_row = row_half[pl.ds(start, tile), :]
    by_row = jnp.concatenate([by_row] * 8, axis=1)
    dlogit = (powers * (by_row + col_half[...])).astype(BF16)
    dlogit_ref[...] = dlogit
    grad = jnp.dot(dlogit, txt_ref[...], preferred_element_type=F32).astype(BF16)
    half = 512 // tile
    mine = (step // half) == core_ref[0]
    inside = pl.multiple_of(lax.rem(step, half) * tile, tile)

    @pl.when(mine)
    def _():
        keep_ref[pl.ds(inside, tile), :] = grad

    @pl.when(jnp.logical_not(mine))
    def _():
        send_ref[pl.ds(inside, tile), :] = grad


def text_kernel(dlogit_ref, img_ref, grad_ref):
    grad_ref[...] = lax.dot_general(
        dlogit_ref[...], img_ref[...], (((0,), (0,)), ((), ())), preferred_element_type=F32
    ).astype(BF16)


def add_kernel(a_ref, b_ref, out_ref):
    out_ref[...] = (a_ref[...].astype(F32) + b_ref[...].astype(F32)).astype(BF16)


def final_kernel(scale_ref, img_ref, txt_ref, img_hat_ref, txt_hat_ref, img_sum_ref, txt_parts_ref, grad_img_ref, grad_txt_ref):
    scale = scale_ref[0]
    txt_sum = jnp.sum(txt_parts_ref[...].astype(F32), axis=0)
    for raw, other, total, out in (
        (img_ref, txt_hat_ref, img_sum_ref[...].astype(F32), grad_img_ref),
        (txt_ref, img_hat_ref, txt_sum, grad_txt_ref),
    ):
        values = raw[...].astype(F32)
        recip = 1.0 / jnp.sqrt(jnp.sum(values * values, axis=1, keepdims=True) + NORM_EPS)
        unit = values * recip
        grad_hat = scale * (total - other[...].astype(F32))
        inner = jnp.sum(grad_hat * unit, axis=1, keepdims=True)
        out[...] = (recip * (grad_hat - unit * inner)).astype(BF16)


def per_device(image_raw, text_raw, log_scale):
    rows, width = image_raw.shape
    total = rows * GROUP
    shape = jax.ShapeDtypeStruct
    img_hat, txt_hat, diag = pl.pallas_call(
        normalize_kernel,
        out_shape=(shape((rows, width), BF16), shape((rows, width), BF16), shape((8, 128), F32)),
        in_specs=[whole()] * 2,
        out_specs=(whole(),) * 3,
        compiler_params=params(),
        name="normalize",
    )(image_raw, text_raw)

    scale = jnp.exp(log_scale[0])
    shift = jnp.maximum(1.01 * scale - 70.0, 0.0)
    scales = jnp.stack([scale, shift])
    core = lax.axis_index("c")
    my_y = lax.axis_index("y")
    my_x = 2 * lax.axis_index("xh") + lax.axis_index("xl")
    near = jnp.array([0, 3, 1, 2], jnp.int32)
    first = jnp.tile(near, 4)
    second = jnp.repeat(near, 4)
    on_x = jnp.where(core == 0, first, second)
    on_y = jnp.where(core == 0, second, first)
    place = ((my_y + on_y) % 4) * 4 + (my_x + on_x) % 4
    core_id = jnp.reshape(core, (1,)).astype(jnp.int32)

    img_all = lax.all_gather(img_hat, LINE, axis=0, tiled=True)
    line = jnp.concatenate(ring_gather(txt_hat, False), axis=0)
    pieces = ring_gather(line, True)

    tile = 256
    steps = total // tile
    fixed = lambda *block: pl.BlockSpec(block, lambda i: (0,) * len(block))
    txt_all, logits, row_part, col_part = pl.pallas_call(
        functools.partial(logits_kernel, tile),
        grid=(steps,),
        out_shape=(
            shape((total, width), BF16),
            shape((total, total), F32),
            shape((16, 128), F32),
            shape((GROUP, 16, 128), F32),
        ),
        in_specs=[whole(pltpu.SMEM), whole(pltpu.SMEM), fixed(total, width)]
        + [fixed(*piece.shape) for piece in pieces],
        out_specs=(
            fixed(total, width),
            pl.BlockSpec((total, tile), lambda i: (0, i)),
            fixed(16, 128),
            fixed(GROUP, 16, 128),
        ),
        scratch_shapes=[pltpu.VMEM((total, width), BF16), pltpu.VMEM((2, total, 128), F32)],
        compiler_params=params(),
        name="logits",
    )(place, scales, img_all, *pieces)

    col_recv = lax.all_to_all(col_part, PLANE, 0, 0, tiled=True)
    row_send, col_sums = pl.pallas_call(
        column_kernel,
        out_shape=(shape((GROUP, 24, 128), F32), shape((8, 128), F32)),
        in_specs=[whole()] * 3,
        out_specs=(whole(),) * 2,
        compiler_params=params(),
        name="columns",
    )(col_recv, row_part, diag)
    row_recv = lax.all_to_all(row_send, LINE, 0, 0, tiled=True)

    keep, send, dlogits, scalars = pl.pallas_call(
        functools.partial(image_kernel, tile),
        grid=(steps,),
        out_shape=(
            shape((total // 2, width), BF16),
            shape((total // 2, width), BF16),
            shape((total, total), BF16),
            shape((8, 128), F32),
        ),
        in_specs=[
            whole(pltpu.SMEM),
            whole(pltpu.SMEM),
            pl.BlockSpec((tile, total), lambda i: (i, 0)),
            fixed(total, width),
            fixed(GROUP, 24, 128),
            fixed(8, 128),
        ],
        out_specs=(
            fixed(total // 2, width),
            fixed(total // 2, width),
            pl.BlockSpec((tile, total), lambda i: (i, 0)),
            fixed(8, 128),
        ),
        scratch_shapes=[pltpu.VMEM((total, 128), F32), pltpu.VMEM((1, total), F32)],
        compiler_params=params(),
        name="image_grad",
    )(core_id, scales, logits, txt_all, row_recv, col_sums)

    sibling = permute(send, lambda x, y, z, c: (x, y, z, c + 1))
    txt_part = pl.pallas_call(
        text_kernel,
        grid=(steps,),
        out_shape=shape((total, width), BF16),
        in_specs=[pl.BlockSpec((total, tile), lambda i: (0, i)), fixed(total, width)],
        out_specs=pl.BlockSpec((tile, width), lambda i: (i, 0)),
        compiler_params=params(),
        cost_estimate=pl.CostEstimate(flops=2 * total * total * width, bytes_accessed=8 << 20, transcendentals=0),
        name="text_grad",
    )(dlogits, img_all)
    both = pl.pallas_call(
        add_kernel,
        out_shape=shape((total // 2, width), BF16),
        in_specs=[whole()] * 2,
        out_specs=whole(),
        compiler_params=params(),
        name="add",
    )(keep, sibling)
    img_sum = lax.psum_scatter(both, "z", scatter_dimension=0, tiled=True)
    txt_parts = lax.all_to_all(jnp.reshape(txt_part, (GROUP, rows, width)), PLANE, 0, 0, tiled=True)

    part = scalars[1:2]
    for along in ("x", "y"):
        moved = [
            permute(part, lambda x, y, z, c, k=k: (x + k, y, z, c) if along == "x" else (x, y + k, z, c))
            for k in (1, 2, 3)
        ]
        part = part + moved[0] + moved[1] + moved[2]

    grad_image, grad_text = pl.pallas_call(
        final_kernel,
        out_shape=(shape((rows, width), BF16),) * 2,
        in_specs=[whole(pltpu.SMEM)] + [whole()] * 6,
        out_specs=(whole(),) * 2,
        compiler_params=params(),
        name="finish",
    )(scales, image_raw, text_raw, img_hat, txt_hat, img_sum, txt_parts)
    batch = total * GROUP
    diag_sum = scale * part[0, 2]
    logs = scalars[0, 0] + part[0, 0] + 2.0 * batch * shift
    loss = (logs - 2.0 * diag_sum) / (2 * batch)
    slope = (scalars[0, 1] + part[0, 1] - diag_sum) / batch
    return grad_image, grad_text, jnp.reshape(loss, (1,)), jnp.reshape(slope, (1,))


def solution(mesh):
    mesh = Mesh(mesh.devices.reshape(SIZES), AXES)
    spec = P(AXES, None)
    return jax.shard_map(
        per_device, mesh=mesh, in_specs=(spec, spec, P()), out_specs=(spec, spec, P(), P()), check_vma=False
    )
```

time: 459 us -> 178 us (0.39)
  the two profiles are of different devices: /device:TPU:16 before, /device:TPU:1 now
where the time goes in v1:
time: 178 us; the launch traced here: 176 us
  waiting for transfers between devices  69.7 us (39%)
  blocking collectives  27.1 us (15%)
  starting transfers between devices  25.7 us (14%)
  Pallas kernels  24.4 us (14%)
  between operations  20.4 us (11%)
  local copies, waits for them, and re-layouts  7.31 us (4%)
    ppermute x15, waiting for transfers between devices, permute(): return lax.ppermute(array, AXES, pairs)  60.1 us
    ppermute x15, starting transfers between devices, permute(): return lax.ppermute(array, AXES, pairs)  21.7 us
    all_to_all x1, blocking collectives, per_device(): row_recv = lax.all_to_all(row_send, LINE, 0, 0, tiled=True)  14 us
    all_to_all x1, blocking collectives, per_device(): col_recv = lax.all_to_all(col_part, PLANE, 0, 0, tiled=True)  13.2 us
    all_gather x1, waiting for transfers between devices, per_device(): img_all = lax.all_gather(img_hat, LINE, axis=0, tiled=True)  9.54 us
    pallas_call x1, Pallas kernels, per_device(): pl.pallas_call(functools.partial(logits_kernel, tile), grid=(steps,), out...  7.55 us
    pallas_call x1, Pallas kernels, per_device(): pl.pallas_call(functools.partial(image_kernel, tile), grid=(steps,), out_...  6.6 us
    unnamed x18, local copies, waits for them, and re-layouts  5.84 us
  transfers between devices with their start and end apart: 18, of which 11 were waited for; matrix products, arithmetic and copies ran while one was open for 1% of the time, Pallas kernels for 3%

profile of v1, /device:TPU:1, one launch (start us, length us, event | category | flops | bytes accessed | tf_op | source)
XLA Modules:
  0.0 175.6 jit_solution(12395541201961035311)
XLA Ops:
  7.2 0.0 all-gather.2.cloned.1.call-start
  7.2 0.0 copy-start.2
  7.2 0.9 copy-done.2
  8.1 0.9 copy-done.4
  9.0 0.9 normalize.1
  9.9 0.0 all-gather.2.cloned.1.call-update
  9.9 0.0 reduce-scatter.2.cloned.1.call-start
  10.0 3.6 %collective-permute-start.1 = (bf16[64,1280]{1,0:T(8,128)(2,1)S(1)}, bf16[64,1280]{1,0:T(8,128)(2,1)S(1)}, u32[]{:S(2)}, u32[]{:S(2)}) collective-permute-start(bf16[64,1280]{1,0:T(8,128)(2,1)S(1)} %get-tuple-element.20.txt_hat_ref), channel_id=1, source_target_pairs={{0,40},{1,41},{2,42},{3,43},{4,44},{5,45},{6,46},{7,47},{8,0},{9,1... | collective-permute-start | bytes 491528 | tf_op jit(solution)/shard_map/ppermute | solution.py:37
  13.6 0.0 collective-permute-start
  13.7 2.2 %collective-permute-done.1 = bf16[64,1280]{1,0:T(8,128)(2,1)S(1)} collective-permute-done((bf16[64,1280]{1,0:T(8,128)(2,1)S(1)}, bf16[64,1280]{1,0:T(8,128)(2,1)S(1)}, u32[]{:S(2)}, u32[]{:S(2)}) %collective-permute-start.1) | collective-permute-done | bytes 163872 | tf_op jit(solution)/shard_map/ppermute | solution.py:37
  15.9 3.1 %collective-permute-start.3 = (bf16[32,1280]{1,0:T(8,128)(2,1)S(1)}, bf16[32,1280]{1,0:T(8,128)(2,1)S(1)}, u32[]{:S(2)}, u32[]{:S(2)}) collective-permute-start(bf16[32,1280]{1,0:T(8,128)(2,1)S(1)} %slice.41), channel_id=1, source_target_pairs={{0,40},{1,41},{2,42},{3,43},{4,44},{5,45},{6,46},{7,47},{8,0},{9,1... | collective-permute-start | bytes 245768 | tf_op jit(solution)/shard_map/ppermute | solution.py:37
  19.0 0.3 collective-permute-done
  19.3 0.0 collective-permute-start.2
  19.4 4.4 %collective-permute-done.2 = bf16[32,1280]{1,0:T(8,128)(2,1)S(1)} collective-permute-done((bf16[32,1280]{1,0:T(8,128)(2,1)S(1)}, bf16[32,1280]{1,0:T(8,128)(2,1)S(1)}, u32[]{:S(2)}, u32[]{:S(2)}) %collective-permute-start.2) | collective-permute-done | bytes 81952 | tf_op jit(solution)/shard_map/ppermute | solution.py:37
  23.8 0.0 collective-permute-done.3
  23.9 2.6 %collective-permute-start.5 = (bf16[256,1280]{1,0:T(8,128)(2,1)S(1)}, bf16[256,1280]{1,0:T(8,128)(2,1)S(1)}, u32[]{:S(2)}, u32[]{:S(2)}) collective-permute-start(bf16[256,1280]{1,0:T(8,128)(2,1)S(1)} %constant_dynamic-update-slice_fusion.t0), channel_id=1, source_target_pairs={{0,192},{1,193},{2,194},{3,195},{4,196},{5,197},{6,198},{7,199},{8... | collective-permute-start | bytes 1966088 | tf_op jit(solution)/shard_map/ppermute | solution.py:37
  26.5 0.0 collective-permute-start.4
  27.2 0.8 select_add_fusion
  28.0 0.1 add.78
  28.1 0.1 add.73
  28.2 5.9 %collective-permute-done.5.t2 = bf16[256,1280]{1,0:T(8,128)(2,1)S(1)} collective-permute-done((bf16[256,1280]{1,0:T(8,128)(2,1)S(1)}, bf16[256,1280]{1,0:T(8,128)(2,1)S(1)}, u32[]{:S(2)}, u32[]{:S(2)}) %collective-permute-start.5) | collective-permute-done | bytes 655392 | tf_op jit(solution)/shard_map/ppermute | solution.py:37
  34.1 3.5 %collective-permute-start.7 = (bf16[128,1280]{1,0:T(8,128)(2,1)S(1)}, bf16[128,1280]{1,0:T(8,128)(2,1)S(1)}, u32[]{:S(2)}, u32[]{:S(2)}) collective-permute-start(bf16[128,1280]{1,0:T(8,128)(2,1)S(1)} %slice.43), channel_id=1, source_target_pairs={{0,192},{1,193},{2,194},{3,195},{4,196},{5,197},{6,198},{7,199},{8... | collective-permute-start | bytes 983048 | tf_op jit(solution)/shard_map/ppermute | solution.py:37
  37.5 0.0 collective-permute-done.4.t1
  37.6 0.1 collective-permute-start.6
  37.7 0.1 pad_maximum_fusion.scale_ref.shift_ref
  37.8 3.8 %collective-permute-done.7.t4 = bf16[128,1280]{1,0:T(8,128)(2,1)S(1)} collective-permute-done((bf16[128,1280]{1,0:T(8,128)(2,1)S(1)}, bf16[128,1280]{1,0:T(8,128)(2,1)S(1)}, u32[]{:S(2)}, u32[]{:S(2)}) %collective-permute-start.7) | collective-permute-done | bytes 327712 | tf_op jit(solution)/shard_map/ppermute | solution.py:37
  41.6 3.6 %collective-permute-done.6.t3 = bf16[128,1280]{1,0:T(8,128)(2,1)S(1)} collective-permute-done((bf16[128,1280]{1,0:T(8,128)(2,1)S(1)}, bf16[128,1280]{1,0:T(8,128)(2,1)S(1)}, u32[]{:S(2)}, u32[]{:S(2)}) %collective-permute-start.6) | collective-permute-done | bytes 327712 | tf_op jit(solution)/shard_map/ppermute | solution.py:37
  45.2 9.5 %all-gather.2.cloned.1.call-done.img_ref = bf16[1024,1280]{1,0:T(8,128)(2,1)} async-done(((bf16[64,1280]{1,0:T(8,128)(2,1)}), bf16[1024,1280]{1,0:T(8,128)(2,1)}) %all-gather.2.cloned.1.call-update) | async-done | bytes 2621456 | tf_op jit(solution)/shard_map/all_gather | solution.py:215
  54.7 7.6 %logits.1 = (bf16[1024,1280]{1,0:T(8,128)(2,1)S(1)}, f32[1024,1024]{1,0:T(8,128)}, f32[16,128]{1,0:T(8,128)S(1)}, f32[16,16,128]{2,1,0:T(8,128)S(1)}) custom-call(s32[16]{0:T(128)S(1)} %fusion.place_ref, f32[2]{0:T(128)S(1)} %pad_maximum_fusion.scale_ref.shift_ref, bf16[1024,1280]{1,0:T(8,128)(2,1)} %all-gather.2.cloned.1.call-done.img_ref, ...), custom_call_target="tpu_custom_call" | custom-call | tf_op jit(solution)/shard_map/logits/pallas_call | solution.py:222
  62.3 0.0 copy-start.1
  62.3 1.6 copy-done.1
  63.9 13.2 %all_to_all.15.col_ref = f32[16,16,128]{2,1,0:T(8,128)S(1)} all-to-all(f32[16,16,128]{2,1,0:T(8,128)S(1)} %get-tuple-element.23), channel_id=1, replica_groups=mesh['y'=4,'xh'=2,'c'=2,'xl'=2,'z'=8] {'y','xh','xl'}, dimensions={0} | all-to-all | bytes 262144 | tf_op jit(solution)/shard_map/all_to_all | solution.py:244
  77.0 0.1 columns.1
  77.2 14.0 %all_to_all.16.recv_ref = f32[16,24,128]{2,1,0:T(8,128)S(1)} all-to-all(f32[16,24,128]{2,1,0:T(8,128)S(1)} %get-tuple-element.26), channel_id=1, replica_groups=mesh['y'=4,'xh'=2,'c'=2,'xl'=2,'z'=8] {'c','z'}, dimensions={0} | all-to-all | bytes 393216 | tf_op jit(solution)/shard_map/all_to_all | solution.py:253
  91.1 6.6 %image_grad.1 = (bf16[512,1280]{1,0:T(8,128)(2,1)S(1)}, bf16[512,1280]{1,0:T(8,128)(2,1)S(1)}, bf16[1024,1024]{1,0:T(8,128)(2,1)S(1)}, f32[8,128]{1,0:T(8,128)S(1)}) custom-call(s32[1]{0:T(128)} %bitcast.2.core_ref, f32[2]{0:T(128)S(1)} %pad_maximum_fusion.scale_ref.shift_ref, f32[1024,1024]{1,0:T(8,128)} %get-tuple-element.21.logit_ref, ...), custom_call_target="tpu_custom_call" | custom-call | tf_op jit(solution)/shard_map/image_grad/pallas_call | solution.py:255
  97.7 1.1 collective-permute-start.8
  98.8 2.7 %collective-permute-done.8.b_ref = bf16[512,1280]{1,0:T(8,128)(2,1)S(1)} collective-permute-done((bf16[512,1280]{1,0:T(8,128)(2,1)S(1)}, bf16[512,1280]{1,0:T(8,128)(2,1)S(1)}, u32[]{:S(2)}, u32[]{:S(2)}) %collective-permute-start.8) | collective-permute-done | bytes 1310752 | tf_op jit(solution)/shard_map/ppermute | solution.py:37
  101.5 1.4 add.112
  102.9 0.0 reduce-scatter.2.cloned.1.call-update
  102.9 5.6 %text_grad.1 = bf16[1024,1280]{1,0:T(8,128)(2,1)S(1)} custom-call(bf16[1024,1024]{1,0:T(8,128)(2,1)S(1)} %get-tuple-element.30.dlogit_ref, bf16[1024,1280]{1,0:T(8,128)(2,1)} %all-gather.2.cloned.1.call-done.img_ref), custom_call_target="tpu_custom_call" | custom-call | flops 2684354560 | bytes 8388608 | tf_op jit(solution)/shard_map/text_grad/pallas_call | solution.py:284
  108.5 0.0 copy-start
  108.5 1.5 copy-done
  110.0 3.9 %all-to-all-start.2 = ((bf16[16,64,1280]{2,1,0:T(8,128)(2,1)}), bf16[16,64,1280]{2,1,0:T(8,128)(2,1)S(1)}, u32[]{:S(2)}, u32[]{:S(2)}) async-start(bf16[16,64,1280]{2,1,0:T(8,128)(2,1)} %bitcast.9), calls=%async_computation.3 | async-start | bytes 5242880 | tf_op jit(solution)/shard_map/all_to_all | solution.py:303
  113.9 3.0 %collective-permute-start.10 = (f32[1,128]{1,0:T(1,128)S(1)}, f32[1,128]{1,0:T(1,128)S(1)}, u32[]{:S(2)}, u32[]{:S(2)}) collective-permute-start(f32[1,128]{1,0:T(1,128)S(1)} %slice.35), channel_id=1, source_target_pairs={{0,32},{1,33},{2,34},{3,35},{4,36},{5,37},{6,38},{7,39},{8,40},{9,... | collective-permute-start | bytes 1544 | tf_op jit(solution)/shard_map/ppermute | solution.py:37
  116.9 0.9 collective-permute-start.11
  117.8 0.6 collective-permute-start.9
  118.3 34.9 %collective-permute-done.10 = f32[1,128]{1,0:T(1,128)S(1)} collective-permute-done((f32[1,128]{1,0:T(1,128)S(1)}, f32[1,128]{1,0:T(1,128)S(1)}, u32[]{:S(2)}, u32[]{:S(2)}) %collective-permute-start.10) | collective-permute-done | bytes 544 | tf_op jit(solution)/shard_map/ppermute | solution.py:37
  153.3 0.0 collective-permute-done.11
  153.3 0.0 collective-permute-done.9
  153.3 1.3 collective-permute-start.14
  154.6 1.1 collective-permute-start.13
  155.7 0.8 collective-permute-start.12
  156.5 0.6 fusion.4
  157.1 0.0 collective-permute-done.14
  157.1 1.4 collective-permute-done.13
  158.5 0.8 collective-permute-done.12
  159.3 0.7 fusion.5
  163.2 0.0 all-to-all-done.2.txt_parts_ref
  163.2 0.0 reduce-scatter.2.cloned.1.call-done.img_sum_ref
  163.2 0.0 copy-done.3
  163.2 0.0 copy-done.5
  163.2 0.0 copy-start.6
  163.2 0.9 copy-done.6
  164.2 2.3 %finish.1 = (bf16[64,1280]{1,0:T(8,128)(2,1)}, bf16[64,1280]{1,0:T(8,128)(2,1)}) custom-call(f32[2]{0:T(128)S(1)} %pad_maximum_fusion.scale_ref.shift_ref, bf16[64,1280]{1,0:T(8,128)(2,1)S(1)} %copy-done.3, bf16[64,1280]{1,0:T(8,128)(2,1)S(1)} %copy-done.5, bf16[64,1280]{1,0:T(8,128)(2,1)} %get-tuple-element.19.img_hat_ref, ...), custom_call_target="tpu_custom_call" | custom-call | tf_op jit(solution)/shard_map/finish/pallas_call | solution.py:313
  (16 shorter events, 0.1 us)
Async XLA Ops:
  7.2 47.6 %all-gather.2.cloned.1.call-start = ((), (), s32[]{:S(2)}) async-start(), calls=%async_computation.4 | async-start | bytes 2785280 | tf_op jit(solution)/shard_map/all_gather | solution.py:215
  7.2 0.9 copy-start.2
  8.1 0.9 copy-start.4
  9.9 153.3 %reduce-scatter.2.cloned.1.call-start = ((), (), s32[]{:S(2)}) async-start(), calls=%async_computation.5 | async-start | bytes 1474560 | tf_op jit(solution)/shard_map/reduce_scatter | solution.py:302
  10.0 5.9 %collective-permute-start.1 = (bf16[64,1280]{1,0:T(8,128)(2,1)S(1)}, bf16[64,1280]{1,0:T(8,128)(2,1)S(1)}, u32[]{:S(2)}, u32[]{:S(2)}) collective-permute-start(bf16[64,1280]{1,0:T(8,128)(2,1)S(1)} %get-tuple-element.20.txt_hat_ref), channel_id=1, source_target_pairs={{0,40},{1,41},{2,42},{3,43},{4,44},{5,45},{6,46},{7,47},{8,0},{9,1... | collective-permute-start | bytes 491528 | tf_op jit(solution)/shard_map/ppermute | solution.py:37
  13.6 5.7 %collective-permute-start = (bf16[64,1280]{1,0:T(8,128)(2,1)S(1)}, bf16[64,1280]{1,0:T(8,128)(2,1)S(1)}, u32[]{:S(2)}, u32[]{:S(2)}) collective-permute-start(bf16[64,1280]{1,0:T(8,128)(2,1)S(1)} %get-tuple-element.20.txt_hat_ref), channel_id=1, source_target_pairs={{0,8},{1,9},{2,10},{3,11},{4,12},{5,13},{6,14},{7,15},{8,32},{9,33... | collective-permute-start | bytes 491528 | tf_op jit(solution)/shard_map/ppermute | solution.py:37
  15.9 7.9 %collective-permute-start.3 = (bf16[32,1280]{1,0:T(8,128)(2,1)S(1)}, bf16[32,1280]{1,0:T(8,128)(2,1)S(1)}, u32[]{:S(2)}, u32[]{:S(2)}) collective-permute-start(bf16[32,1280]{1,0:T(8,128)(2,1)S(1)} %slice.41), channel_id=1, source_target_pairs={{0,40},{1,41},{2,42},{3,43},{4,44},{5,45},{6,46},{7,47},{8,0},{9,1... | collective-permute-start | bytes 245768 | tf_op jit(solution)/shard_map/ppermute | solution.py:37
  19.3 4.5 %collective-permute-start.2 = (bf16[32,1280]{1,0:T(8,128)(2,1)S(1)}, bf16[32,1280]{1,0:T(8,128)(2,1)S(1)}, u32[]{:S(2)}, u32[]{:S(2)}) collective-permute-start(bf16[32,1280]{1,0:T(8,128)(2,1)S(1)} %slice.40), channel_id=1, source_target_pairs={{0,8},{1,9},{2,10},{3,11},{4,12},{5,13},{6,14},{7,15},{8,32},{9,33... | collective-permute-start | bytes 245768 | tf_op jit(solution)/shard_map/ppermute | solution.py:37
  23.9 10.2 %collective-permute-start.5 = (bf16[256,1280]{1,0:T(8,128)(2,1)S(1)}, bf16[256,1280]{1,0:T(8,128)(2,1)S(1)}, u32[]{:S(2)}, u32[]{:S(2)}) collective-permute-start(bf16[256,1280]{1,0:T(8,128)(2,1)S(1)} %constant_dynamic-update-slice_fusion.t0), channel_id=1, source_target_pairs={{0,192},{1,193},{2,194},{3,195},{4,196},{5,197},{6,198},{7,199},{8... | collective-permute-start | bytes 1966088 | tf_op jit(solution)/shard_map/ppermute | solution.py:37
  26.5 11.0 %collective-permute-start.4 = (bf16[256,1280]{1,0:T(8,128)(2,1)S(1)}, bf16[256,1280]{1,0:T(8,128)(2,1)S(1)}, u32[]{:S(2)}, u32[]{:S(2)}) collective-permute-start(bf16[256,1280]{1,0:T(8,128)(2,1)S(1)} %constant_dynamic-update-slice_fusion.t0), channel_id=1, source_target_pairs={{0,64},{1,65},{2,66},{3,67},{4,68},{5,69},{6,70},{7,71},{8,72},{9,... | collective-permute-start | bytes 1966088 | tf_op jit(solution)/shard_map/ppermute | solution.py:37
  34.1 7.5 %collective-permute-start.7 = (bf16[128,1280]{1,0:T(8,128)(2,1)S(1)}, bf16[128,1280]{1,0:T(8,128)(2,1)S(1)}, u32[]{:S(2)}, u32[]{:S(2)}) collective-permute-start(bf16[128,1280]{1,0:T(8,128)(2,1)S(1)} %slice.43), channel_id=1, source_target_pairs={{0,192},{1,193},{2,194},{3,195},{4,196},{5,197},{6,198},{7,199},{8... | collective-permute-start | bytes 983048 | tf_op jit(solution)/shard_map/ppermute | solution.py:37
  37.6 7.6 %collective-permute-start.6 = (bf16[128,1280]{1,0:T(8,128)(2,1)S(1)}, bf16[128,1280]{1,0:T(8,128)(2,1)S(1)}, u32[]{:S(2)}, u32[]{:S(2)}) collective-permute-start(bf16[128,1280]{1,0:T(8,128)(2,1)S(1)} %slice.42), channel_id=1, source_target_pairs={{0,64},{1,65},{2,66},{3,67},{4,68},{5,69},{6,70},{7,71},{8,72},{9,... | collective-permute-start | bytes 983048 | tf_op jit(solution)/shard_map/ppermute | solution.py:37
  62.3 1.6 copy-start.1
  97.7 3.7 %collective-permute-start.8 = (bf16[512,1280]{1,0:T(8,128)(2,1)S(1)}, bf16[512,1280]{1,0:T(8,128)(2,1)S(1)}, u32[]{:S(2)}, u32[]{:S(2)}) collective-permute-start(bf16[512,1280]{1,0:T(8,128)(2,1)S(1)} %get-tuple-element.29), channel_id=1, source_target_pairs={{0,16},{1,17},{2,18},{3,19},{4,20},{5,21},{6,22},{7,23},{8,24},{9,... | collective-permute-start | bytes 3932168 | tf_op jit(solution)/shard_map/ppermute | solution.py:37
  108.5 1.5 copy-start
  110.0 53.2 %copy-start.3 = (bf16[64,1280]{1,0:T(8,128)(2,1)S(1)}, bf16[64,1280]{1,0:T(8,128)(2,1)}, u32[]{:S(2)}) copy-start(bf16[64,1280]{1,0:T(8,128)(2,1)} %img_ref.3) | copy-start | bytes 491524
  110.0 53.3 %copy-start.5 = (bf16[64,1280]{1,0:T(8,128)(2,1)S(1)}, bf16[64,1280]{1,0:T(8,128)(2,1)}, u32[]{:S(2)}) copy-start(bf16[64,1280]{1,0:T(8,128)(2,1)} %txt_ref.3) | copy-start | bytes 491524
  110.0 53.2 %all-to-all-start.2 = ((bf16[16,64,1280]{2,1,0:T(8,128)(2,1)}), bf16[16,64,1280]{2,1,0:T(8,128)(2,1)S(1)}, u32[]{:S(2)}, u32[]{:S(2)}) async-start(bf16[16,64,1280]{2,1,0:T(8,128)(2,1)} %bitcast.9), calls=%async_computation.3 | async-start | bytes 5242880 | tf_op jit(solution)/shard_map/all_to_all | solution.py:303
  113.9 39.4 %collective-permute-start.10 = (f32[1,128]{1,0:T(1,128)S(1)}, f32[1,128]{1,0:T(1,128)S(1)}, u32[]{:S(2)}, u32[]{:S(2)}) collective-permute-start(f32[1,128]{1,0:T(1,128)S(1)} %slice.35), channel_id=1, source_target_pairs={{0,32},{1,33},{2,34},{3,35},{4,36},{5,37},{6,38},{7,39},{8,40},{9,... | collective-permute-start | bytes 1544 | tf_op jit(solution)/shard_map/ppermute | solution.py:37
  116.9 36.4 %collective-permute-start.11 = (f32[1,128]{1,0:T(1,128)S(1)}, f32[1,128]{1,0:T(1,128)S(1)}, u32[]{:S(2)}, u32[]{:S(2)}) collective-permute-start(f32[1,128]{1,0:T(1,128)S(1)} %slice.35), channel_id=1, source_target_pairs={{0,40},{1,41},{2,42},{3,43},{4,44},{5,45},{6,46},{7,47},{8,0},{9,1... | collective-permute-start | bytes 1544 | tf_op jit(solution)/shard_map/ppermute | solution.py:37
  117.8 35.5 %collective-permute-start.9 = (f32[1,128]{1,0:T(1,128)S(1)}, f32[1,128]{1,0:T(1,128)S(1)}, u32[]{:S(2)}, u32[]{:S(2)}) collective-permute-start(f32[1,128]{1,0:T(1,128)S(1)} %slice.35), channel_id=1, source_target_pairs={{0,8},{1,9},{2,10},{3,11},{4,12},{5,13},{6,14},{7,15},{8,32},{9,33... | collective-permute-start | bytes 1544 | tf_op jit(solution)/shard_map/ppermute | solution.py:37
  153.3 3.8 %collective-permute-start.14 = (f32[1,128]{1,0:T(1,128)S(1)}, f32[1,128]{1,0:T(1,128)S(1)}, u32[]{:S(2)}, u32[]{:S(2)}) collective-permute-start(f32[1,128]{1,0:T(1,128)S(1)} %add_add_fusion.1), channel_id=1, source_target_pairs={{0,192},{1,193},{2,194},{3,195},{4,196},{5,197},{6,198},{7,199},{8... | collective-permute-start | bytes 1544 | tf_op jit(solution)/shard_map/ppermute | solution.py:37
  154.6 3.9 %collective-permute-start.13 = (f32[1,128]{1,0:T(1,128)S(1)}, f32[1,128]{1,0:T(1,128)S(1)}, u32[]{:S(2)}, u32[]{:S(2)}) collective-permute-start(f32[1,128]{1,0:T(1,128)S(1)} %add_add_fusion.1), channel_id=1, source_target_pairs={{0,128},{1,129},{2,130},{3,131},{4,132},{5,133},{6,134},{7,135},{8... | collective-permute-start | bytes 1544 | tf_op jit(solution)/shard_map/ppermute | solution.py:37
  155.7 3.6 %collective-permute-start.12 = (f32[1,128]{1,0:T(1,128)S(1)}, f32[1,128]{1,0:T(1,128)S(1)}, u32[]{:S(2)}, u32[]{:S(2)}) collective-permute-start(f32[1,128]{1,0:T(1,128)S(1)} %add_add_fusion.1), channel_id=1, source_target_pairs={{0,64},{1,65},{2,66},{3,67},{4,68},{5,69},{6,70},{7,71},{8,72},{9,... | collective-permute-start | bytes 1544 | tf_op jit(solution)/shard_map/ppermute | solution.py:37
  163.2 0.9 copy-start.6
Sparse Core Ops, SparseCore 0:
  10.1 44.6 all-gather.1
  103.0 29.9 reduce-scatter.1
